TPU v7x, 32 devices: a whole 2x2x4 slice. The times are simulated.
32 devices in a mesh: grp: 2 (over y), tile: 4 (over z), shot: 2 (over x), gz: 2 (over core).
Axes of the slice: x: 2, y: 2, z: 4, core: 2. Of those that a mesh axis runs over, the one named last changes fastest.
Arguments:
- courant: float32 [128, 32, 256], P('tile', None, 'gz'), may hold values from 0.2 to 0.44
- forward_old: float32 [4, 128, 32, 256], P(('grp', 'shot'), 'tile', None, 'gz'), parts along dimension 0, may hold values from -6 to 6
- forward_now: float32 [4, 128, 32, 256], P(('grp', 'shot'), 'tile', None, 'gz'), parts along dimension 0, may hold values from -6 to 6
- adjoint_far: float32 [4, 128, 32, 256], P(('grp', 'shot'), 'tile', None, 'gz'), parts along dimension 0, may hold values from -6 to 6
- adjoint_near: float32 [4, 128, 32, 256], P(('grp', 'shot'), 'tile', None, 'gz'), parts along dimension 0, may hold values from -6 to 6
- wavelet: float32 [256], replicated, may hold values from 200 to 800
- source_cell: int32 [4], P(('grp', 'shot')), parts along dimension 0, may hold values from 0 to 1048575
- checkpoint_step: int32 [4], P(('grp', 'shot')), parts along dimension 0, may hold values from 0 to 255
- receiver_cell: int32 [4, 512], P(('grp', 'shot')), parts along dimension 0, may hold values from 0 to 1048575
- residual: float32 [4, 2, 512], P(('grp', 'shot')), parts along dimension 0, may hold values from -80 to 80
- weight_table: float32 [16], replicated, may hold values from 0.25 to 4
- weight_index: int32 [4], P(('grp', 'shot')), parts along dimension 0, may hold values from 0 to 15
Outputs:
- gradient: float32 [256, 32, 256], P(('grp', 'tile'), 'shot', 'gz'), parts along dimension 0
- illumination: float32 [256, 32, 256], P(('grp', 'tile'), 'shot', 'gz'), parts along dimension 0
- adjoint_now: float32 [4, 128, 32, 256], P(('grp', 'shot'), 'tile', None, 'gz'), parts along dimension 0
- adjoint_back: float32 [4, 128, 32, 256], P(('grp', 'shot'), 'tile', None, 'gz'), parts along dimension 0
There are 2 independent parts, one for each index of `grp`. A program takes and returns all parts, laid end to end along the dimension named above; an argument that names none is the same for every part. Nothing has to cross between parts.
All inputs are finite; a program needn't handle non-finite values.
Results may differ from a plain program's by a relative error of at most 0.00002.
Values sent between devices are 32-bit elements; how exact they have to be, the bound alone decides.
A program may use at most 64 MiB of HBM per device.

v0:
```python
import jax
import jax.numpy as jnp
from jax import lax
from jax.sharding import PartitionSpec as P

STENCIL = (-205.0 / 72.0, 8.0 / 5.0, -1.0 / 5.0, 8.0 / 315.0, -1.0 / 560.0)


def padded_2(x, sides, width):
    for axis, dim in sides:
        count, length = (lax.axis_size(axis), x.shape[dim])
        up = [(i, (i + 1) % count) for i in range(count - 1)]
        down = [(j, i) for i, j in up]
        last = lax.slice_in_dim(x, length - width, length, axis=dim)
        initial = lax.slice_in_dim(x, 0, width, axis=dim)
        before = lax.ppermute(last, axis, up)
        after = lax.ppermute(initial, axis, down)
        x = jnp.concatenate([before, x, after], axis=dim)
    return x


def laplace_padded(padded, extent_x, extent_y, extent_z):
    center = padded[:, 4 : 4 + extent_x, 4 : 4 + extent_y, 4 : 4 + extent_z]
    summed = 3.0 * STENCIL[0] * center
    for offset in range(1, 5):
        near_x = (
            padded[:, 4 + offset : 4 + offset + extent_x, 4 : 4 + extent_y, 4 : 4 + extent_z]
            + padded[:, 4 - offset : 4 - offset + extent_x, 4 : 4 + extent_y, 4 : 4 + extent_z]
        )
        near_y = (
            padded[:, 4 : 4 + extent_x, 4 + offset : 4 + offset + extent_y, 4 : 4 + extent_z]
            + padded[:, 4 : 4 + extent_x, 4 - offset : 4 - offset + extent_y, 4 : 4 + extent_z]
        )
        near_z = (
            padded[:, 4 : 4 + extent_x, 4 : 4 + extent_y, 4 + offset : 4 + offset + extent_z]
            + padded[:, 4 : 4 + extent_x, 4 : 4 + extent_y, 4 - offset : 4 - offset + extent_z]
        )
        summed = summed + STENCIL[offset] * (near_x + near_y + near_z)
    return summed


def shards(
    courant,
    forward_old,
    forward_now,
    adjoint_far,
    adjoint_near,
    wavelet,
    source_cell,
    checkpoint_step,
    receiver_cell,
    residual,
    weight_table,
    weight_index,
):
    shots_here, extent_x, extent_y, extent_z = forward_now.shape
    block_cells = extent_x * extent_y * extent_z
    total_z = extent_z * lax.axis_size("gz")
    start_x = lax.axis_index("tile") * extent_x
    start_z = lax.axis_index("gz") * extent_z
    shots_all = shots_here * lax.axis_size("shot")
    speed_sq = courant * courant

    def spread(flat_cells, values):
        coord_x = flat_cells // (extent_y * total_z)
        coord_y = flat_cells // total_z % extent_y
        coord_z = flat_cells % total_z
        local_x = coord_x - start_x
        local_z = coord_z - start_z
        inside = (local_x >= 0) & (local_x < extent_x) & (local_z >= 0) & (local_z < extent_z)
        shot_offset = (jnp.arange(shots_here, dtype=jnp.int32) * block_cells)[:, None]
        target = jnp.where(
            inside,
            (local_x * extent_y + coord_y) * extent_z + local_z + shot_offset,
            shots_here * block_cells,
        )
        grid = (
            jnp.zeros((shots_here * block_cells,), jnp.float32)
            .at[target.reshape(-1)]
            .add(values.reshape(-1), mode="drop")
        )
        return grid.reshape(shots_here, extent_x, extent_y, extent_z)

    def laplace_pair(leading, second):
        joined = jnp.concatenate([leading, second], axis=0)
        padded = padded_2(joined, (("tile", 1), ("gz", 3)), 4)
        padded = jnp.pad(padded, ((0, 0), (0, 0), (4, 4), (0, 0)))
        result = laplace_padded(padded, extent_x, extent_y, extent_z)
        return (result[:shots_here], result[shots_here:])

    table_match = (
        weight_index[:, None] == jnp.arange(weight_table.shape[0], dtype=jnp.int32)[None, :]
    )
    weights = jnp.sum(jnp.where(table_match, weight_table[None, :], 0.0), axis=1)
    step_match = checkpoint_step[:, None] == jnp.arange(wavelet.shape[0], dtype=jnp.int32)[None, :]
    amplitude = jnp.sum(jnp.where(step_match, wavelet[None, :], 0.0), axis=1)
    source_grid = spread(source_cell[:, None], amplitude[:, None])
    shot_scale = weights[:, None, None, None]
    lap_now, lap_near = laplace_pair(forward_now, adjoint_near)
    forward_next = 2.0 * forward_now - forward_old + speed_sq * (lap_now + source_grid)
    adjoint_now = (
        2.0 * adjoint_near
        - adjoint_far
        + speed_sq * (lap_near + spread(receiver_cell, residual[:, 0]))
    )
    early_grad = jnp.sum(shot_scale * 2.0 * courant * (adjoint_now * lap_now), axis=0)
    early_energy = jnp.sum(shot_scale * (forward_now * forward_now), axis=0)
    early_sums = (
        lax.psum_scatter(early_grad, "shot", scatter_dimension=1, tiled=True),
        lax.psum_scatter(early_energy, "shot", scatter_dimension=1, tiled=True),
    )
    lap_next, lap_adjoint = laplace_pair(forward_next, adjoint_now)
    adjoint_back = (
        2.0 * adjoint_now
        - adjoint_near
        + speed_sq * (lap_adjoint + spread(receiver_cell, residual[:, 1]))
    )
    late_grad = jnp.sum(shot_scale * 2.0 * courant * (adjoint_near * lap_next), axis=0)
    late_energy = jnp.sum(shot_scale * (forward_next * forward_next), axis=0)
    late_sums = (
        lax.psum_scatter(late_grad, "shot", scatter_dimension=1, tiled=True),
        lax.psum_scatter(late_energy, "shot", scatter_dimension=1, tiled=True),
    )
    gradient = (early_sums[0] + late_sums[0]) / shots_all
    illumination = (early_sums[1] + late_sums[1]) / shots_all
    return (gradient, illumination, adjoint_now, adjoint_back)


def solution(mesh):
    in_specs = (
        P("tile", None, "gz"),
        P(("grp", "shot"), "tile", None, "gz"),
        P(("grp", "shot"), "tile", None, "gz"),
        P(("grp", "shot"), "tile", None, "gz"),
        P(("grp", "shot"), "tile", None, "gz"),
        P(),
        P(("grp", "shot")),
        P(("grp", "shot")),
        P(("grp", "shot"), None),
        P(("grp", "shot"), None, None),
        P(),
        P(("grp", "shot")),
    )
    out_specs = (
        P(("grp", "tile"), "shot", "gz"),
        P(("grp", "tile"), "shot", "gz"),
        P(("grp", "shot"), "tile", None, "gz"),
        P(("grp", "shot"), "tile", None, "gz"),
    )
    return jax.shard_map(shards, mesh=mesh, in_specs=in_specs, out_specs=out_specs, check_vma=False)
```

profile of v0, /device:TPU:0, one launch (start us, length us, event | category | flops | bytes accessed | tf_op | source)
XLA Modules:
  0.0 133.7 jit_solution(2549004247985901916)
XLA Ops:
  9.4 4.9 %collective-permute-start.1 = (f32[2,4,32,128]{3,2,1,0:T(8,128)S(1)}, f32[2,4,32,128]{3,2,1,0:T(8,128)S(1)}, u32[]{:S(2)}, u32[]{:S(2)}) collective-permute-start(f32[2,4,32,128]{3,2,1,0:T(8,128)S(1)} %get-tuple-element.38), channel_id=1, source_target_pairs={{0,4},{4,8},{8,12},{1,5},{5,9},{9,13},{2,6},{6,10},{10,14},{3,7},{... | collective-permute-start | bytes 393224 | tf_op jit(solution)/shard_map/ppermute | solution.py:16
  14.4 1.3 collective-permute-start
  17.8 3.5 %collective-permute-done = f32[2,4,32,128]{3,2,1,0:T(8,128)S(1)} collective-permute-done((f32[2,4,32,128]{3,2,1,0:T(8,128)S(1)}, f32[2,4,32,128]{3,2,1,0:T(8,128)S(1)}, u32[]{:S(2)}, u32[]{:S(2)}) %collective-permute-start) | collective-permute-done | bytes 131104 | tf_op jit(solution)/shard_map/ppermute | solution.py:17
  21.3 1.5 %fusion.66 = (f32[2,40,32,4]{3,2,1,0:T(8,128)}, f32[2,40,32,4]{3,2,1,0:T(8,128)S(1)}) fusion(f32[2,40,32,128]{3,2,1,0:T(8,128)S(1)} %pad_maximum_fusion.3), kind=kLoop, calls=%fused_computation.151 | loop fusion | bytes 163840 | tf_op jit(solution)/shard_map/slice | solution.py:15
  22.9 2.0 %copy.34 = f32[2,40,32,4]{1,2,3,0:T(8,128)S(1)} copy(f32[2,40,32,4]{3,2,1,0:T(8,128)} %get-tuple-element.31) | data formatting | bytes 81920 | tf_op jit(solution)/shard_map/slice | solution.py:15
  24.9 1.3 collective-permute-start.3
  27.0 3.0 %collective-permute-start.2 = (f32[2,40,32,4]{1,2,3,0:T(8,128)S(1)}, f32[2,40,32,4]{1,2,3,0:T(8,128)S(1)}, u32[]{:S(2)}, u32[]{:S(2)}) collective-permute-start(f32[2,40,32,4]{1,2,3,0:T(8,128)S(1)} %copy.33), channel_id=1, source_target_pairs={{0,1},{2,3},{4,5},{6,7},{8,9},{10,11},{12,13},{14,15},{16,17},{18,... | collective-permute-start | bytes 122888 | tf_op jit(solution)/shard_map/ppermute | solution.py:16
  31.9 4.0 %scatter_custom_fusion = f32[131072]{0:T(1024)} fusion(s32[512]{0:T(512)S(1)} %bitcast.41, f32[512]{0:T(512)S(1)} %bitcast.44, f32[]{:T(128)} %constant.148.clone.1), kind=kCustom, calls=%fused_computation.119 | custom fusion | flops 512 | bytes 524292 | tf_op jit(solution)/shard_map/scatter-add | solution.py:80
  36.0 1.4 %fusion.63 = f32[131072]{0:T(1024)S(1)} fusion(f32[131072]{0:T(1024)S(1)} %broadcast.117, s32[]{:T(128)} %bitcast.13, f32[1]{0:T(128)} %bitcast.12, s32[1,1]{1,0:T(1,128)S(6)} %select_n.87), kind=kLoop, calls=%fused_computation.149 | loop fusion | flops 7 | bytes 524 | tf_op jit(solution)/shard_map/scatter-add | solution.py:80
  39.4 2.2 %copy.35 = f32[2,40,32,4]{3,2,1,0:T(8,128)} copy(f32[2,40,32,4]{1,2,3,0:T(8,128)S(1)} %collective-permute-done.2) | data formatting | bytes 81920 | tf_op jit(solution)/shard_map/ppermute | solution.py:16
  41.6 4.6 %pad_maximum_fusion = (f32[2,40,32,132]{3,2,1,0:T(8,128)}, f32[2,40,32,132]{3,2,1,0:T(8,128)}) fusion(f32[2,40,32,4]{3,2,1,0:T(8,128)S(1)} %copy.36, f32[2,4,32,128]{3,2,1,0:T(8,128)S(1)} %collective-permute-done, f32[2,32,32,128]{3,2,1,0:T(8,128)S(1)} %constant_dynamic-update-slice_fusion, f32[2,4,32,128]{3,2,1,0:T(8,128)S(1)} %collective-permute-done.1, ...), kind=kLoop, calls=%fused_computation.14 | loop fusion | flops 2027520 | bytes 4096000 | tf_op jit(solution)/shard_map/concatenate | solution.py:18
  46.2 2.1 %select_maximum_fusion.5 = f32[2,40,40,136]{3,2,1,0:T(8,128)S(1)} fusion(f32[2,40,32,4]{3,2,1,0:T(8,128)S(1)} %copy.36, f32[2,40,32,4]{3,2,1,0:T(8,128)S(1)} %copy-done.3, f32[2,4,32,128]{3,2,1,0:T(8,128)S(1)} %collective-permute-done, f32[2,32,32,128]{3,2,1,0:T(8,128)S(1)} %constant_dynamic-update-slice_fusion, f32[2,4,32,128]{3,2,1,0:T(8,128)S(1)} %collective-permute-done.1), kind=kLoop, calls=%fused_computation.9 | loop fusion | flops 5222400 | bytes 3133440 | tf_op jit(solution)/shard_map/concatenate | solution.py:18
  48.3 10.4 %fusion.7 = f32[2,32,32,128]{3,2,1,0:T(8,128)S(1)} fusion(f32[2,32,32,128]{3,2,1,0:T(8,128)S(1)} %constant_dynamic-update-slice_fusion, f32[2,4,32,128]{3,2,1,0:T(8,128)S(1)} %collective-permute-done.1, f32[2,4,32,128]{3,2,1,0:T(8,128)S(1)} %collective-permute-done, f32[2,40,32,132]{3,2,1,0:T(8,128)} %get-tuple-element.30, ...), kind=kLoop, calls=%fused_computation.45 | loop fusion | flops 9699328 | bytes 19136512 | tf_op jit(solution)/shard_map/add | solution.py:38
  58.7 3.7 %multiply_bitcast_fusion = (f32[32,32,128]{2,1,0:T(8,128)}, f32[1,32,32,128]{3,2,1,0:T(8,128)S(1)}, f32[1,32,32,128]{3,2,1,0:T(8,128)S(1)}) fusion(f32[1,32,32,128]{3,2,1,0:T(8,128)} %param.16, f32[]{:T(128)} %fusion.62, f32[1,32,32,128]{3,2,1,0:T(8,128)} %bitcast.40, f32[2,32,32,128]{3,2,1,0:T(8,128)S(1)} %fusion.7, f32[32,32,128]{2,1,0:T(8,128)S(1)} %copy-done.8, ...), kind=kLoop, calls=%fused_computation.114 | loop fusion | flops 1966080 | bytes 6291460 | tf_op jit(solution)/shard_map/add | solution.py:125
  62.5 1.3 collective-permute-start.4
  63.8 4.6 %collective-permute-start.5 = (f32[2,4,32,128]{3,2,1,0:T(8,128)S(1)}, f32[2,4,32,128]{3,2,1,0:T(8,128)S(1)}, u32[]{:S(2)}, u32[]{:S(2)}) collective-permute-start(f32[2,4,32,128]{3,2,1,0:T(8,128)S(1)} %get-tuple-element.35), channel_id=1, source_target_pairs={{0,4},{4,8},{8,12},{1,5},{5,9},{9,13},{2,6},{6,10},{10,14},{3,7},{... | collective-permute-start | bytes 393224 | tf_op jit(solution)/shard_map/ppermute | solution.py:16
  68.3 4.0 %scatter_custom_fusion.1 = f32[131072]{0:T(1024)} fusion(s32[512]{0:T(512)S(1)} %bitcast.42, f32[512]{0:T(512)S(1)} %bitcast.43, f32[]{:T(128)} %constant.148.clone.1), kind=kCustom, calls=%fused_computation.117 | custom fusion | flops 512 | bytes 524292 | tf_op jit(solution)/shard_map/scatter-add | solution.py:80
  73.9 1.5 %fusion.65 = (f32[2,40,32,4]{3,2,1,0:T(8,128)}, f32[2,40,32,4]{3,2,1,0:T(8,128)S(1)}) fusion(f32[2,40,32,128]{3,2,1,0:T(8,128)S(1)} %pad_maximum_fusion.4), kind=kLoop, calls=%fused_computation.150 | loop fusion | bytes 163840 | tf_op jit(solution)/shard_map/slice | solution.py:15
  75.5 2.7 %copy.40 = f32[2,40,32,4]{1,2,3,0:T(8,128)} copy(f32[2,40,32,4]{3,2,1,0:T(8,128)} %get-tuple-element.27) | data formatting | bytes 81920 | tf_op jit(solution)/shard_map/slice | solution.py:15
  78.1 1.3 collective-permute-start.7
  79.4 1.4 %copy.39 = f32[2,40,32,4]{1,2,3,0:T(8,128)} copy(f32[2,40,32,4]{3,2,1,0:T(8,128)S(1)} %get-tuple-element.28) | data formatting | bytes 81920 | tf_op jit(solution)/shard_map/slice | solution.py:14
  80.8 4.3 %collective-permute-start.6 = (f32[2,40,32,4]{1,2,3,0:T(8,128)}, f32[2,40,32,4]{1,2,3,0:T(8,128)}, u32[]{:S(2)}, u32[]{:S(2)}) collective-permute-start(f32[2,40,32,4]{1,2,3,0:T(8,128)} %copy.39), channel_id=1, source_target_pairs={{0,1},{2,3},{4,5},{6,7},{8,9},{10,11},{12,13},{14,15},{16,17},{18,... | collective-permute-start | bytes 122888 | tf_op jit(solution)/shard_map/ppermute | solution.py:16
  85.1 1.2 pad_maximum_fusion.5
  86.4 3.0 %copy.42 = f32[2,40,32,4]{3,2,1,0:T(8,128)} copy(f32[2,40,32,4]{1,2,3,0:T(8,128)} %collective-permute-done.7) | data formatting | bytes 81920 | tf_op jit(solution)/shard_map/ppermute | solution.py:17
  89.4 3.0 %copy.41 = f32[2,40,32,4]{3,2,1,0:T(8,128)} copy(f32[2,40,32,4]{1,2,3,0:T(8,128)} %collective-permute-done.6) | data formatting | bytes 81920 | tf_op jit(solution)/shard_map/ppermute | solution.py:16
  92.4 4.0 %pad_maximum_fusion.1 = (f32[2,40,32,132]{3,2,1,0:T(8,128)S(1)}, f32[2,40,32,132]{3,2,1,0:T(8,128)}) fusion(f32[2,40,32,4]{3,2,1,0:T(8,128)} %copy.42, f32[2,4,32,128]{3,2,1,0:T(8,128)S(1)} %collective-permute-done.4, f32[1,32,32,128]{3,2,1,0:T(8,128)S(1)} %get-tuple-element.24, f32[1,32,32,128]{3,2,1,0:T(8,128)S(1)} %get-tuple-element.21, ...), kind=kLoop, calls=%fused_computation.16 | loop fusion | flops 2703360 | bytes 4096000 | tf_op jit(solution)/shard_map/concatenate | solution.py:18
  96.5 3.1 %select_maximum_fusion = f32[2,40,40,136]{3,2,1,0:T(8,128)S(1)} fusion(f32[2,40,32,4]{3,2,1,0:T(8,128)S(1)} %copy-done.1, f32[2,40,32,4]{3,2,1,0:T(8,128)S(1)} %copy-done.2, f32[2,4,32,128]{3,2,1,0:T(8,128)S(1)} %collective-permute-done.4, f32[2,4,32,128]{3,2,1,0:T(8,128)S(1)} %copy-done.7, f32[1,32,32,128]{3,2,1,0:T(8,128)S(1)} %get-tuple-element.24, ...), kind=kLoop, calls=%fused_computation.4 | loop fusion | flops 6092800 | bytes 3133440 | tf_op jit(solution)/shard_map/concatenate | solution.py:18
  99.6 7.5 %fusion.27 = f32[2,32,32,128]{3,2,1,0:T(8,128)} fusion(f32[1,32,32,128]{3,2,1,0:T(8,128)S(1)} %get-tuple-element.24, f32[1,32,32,128]{3,2,1,0:T(8,128)S(1)} %get-tuple-element.21, f32[2,40,32,132]{3,2,1,0:T(8,128)} %get-tuple-element.26, f32[2,40,32,132]{3,2,1,0:T(8,128)S(1)} %get-tuple-element.25, f32[2,40,40,136]{3,2,1,0:T(8,128)S(1)} %select_maximum_fusion, ...), kind=kLoop, calls=%fused_computation.65 | loop fusion | flops 7864320 | bytes 27262976 | tf_op jit(solution)/shard_map/add | solution.py:38
  107.0 3.2 %fusion.45 = (f32[1,32,32,128]{3,2,1,0:T(8,128)}, f32[32,32,128]{2,1,0:T(8,128)}) fusion(f32[1,32,32,128]{3,2,1,0:T(8,128)} %bitcast.38, f32[2,32,32,128]{3,2,1,0:T(8,128)} %fusion.27, f32[1,32,32,128]{3,2,1,0:T(8,128)} %param.18, f32[1,32,32,128]{3,2,1,0:T(8,128)S(1)} %get-tuple-element.24, f32[32,32,128]{2,1,0:T(8,128)} %param.14, f32[]{:T(128)S(6)} %mul.123, ...), kind=kLoop, calls=%fused_computation.106 | loop fusion | flops 1441792 | bytes 4718596 | tf_op jit(solution)/shard_map/add | solution.py:114
  110.3 1.7 %broadcast_multiply_fusion = f32[32,16,128]{2,1,0:T(8,128)} fusion(f32[32,16,128]{2,1,0:T(8,128)} %reduce-scatter.5.cloned.1.call-done), kind=kLoop, calls=%fused_computation.123 | loop fusion | flops 65536 | bytes 524288 | tf_op jit(solution)/shard_map/div | solution.py:125
  112.0 13.2 %reduce-scatter.3.cloned.1.call-done = f32[32,16,128]{2,1,0:T(8,128)} async-done(((f32[32,32,128]{2,1,0:T(8,128)}), f32[32,16,128]{2,1,0:T(8,128)}) %reduce-scatter.3.cloned.1.call-update) | async-done | bytes 262160 | tf_op jit(solution)/shard_map/reduce_scatter | solution.py:109
  125.2 1.7 %broadcast_multiply_fusion.1 = f32[32,16,128]{2,1,0:T(8,128)} fusion(f32[32,16,128]{2,1,0:T(8,128)} %reduce-scatter.3.cloned.1.call-done), kind=kLoop, calls=%fused_computation.124 | loop fusion | flops 65536 | bytes 524288 | tf_op jit(solution)/shard_map/div | solution.py:124
  (54 shorter events, 7.9 us)
Async XLA Ops:
  7.2 8.5 %copy-start.10 = (f32[1,2,512]{2,1,0:T(2,128)S(1)}, f32[1,2,512]{2,1,0:T(2,128)}, u32[]{:S(2)}) copy-start(f32[1,2,512]{2,1,0:T(2,128)} %param.23) | copy-start | bytes 12292
  7.2 8.5 %copy-start.11 = (s32[1,512]{1,0:T(1,128)S(1)}, s32[1,512]{1,0:T(1,128)}, u32[]{:S(2)}) copy-start(s32[1,512]{1,0:T(1,128)} %param.22) | copy-start | bytes 6148
  7.2 9.9 %copy-start.12 = (f32[256]{0:T(256)S(1)}, f32[256]{0:T(256)}, u32[]{:S(2)}) copy-start(f32[256]{0:T(256)} %param.19) | copy-start | bytes 3076
  7.2 103.1 %reduce-scatter.5.cloned.1.call-start = ((), (), s32[]{:S(2)}) async-start(), calls=%async_computation.3 | async-start | bytes 786432 | tf_op jit(solution)/shard_map/reduce_scatter | solution.py:110
  9.4 8.3 %collective-permute-start.1 = (f32[2,4,32,128]{3,2,1,0:T(8,128)S(1)}, f32[2,4,32,128]{3,2,1,0:T(8,128)S(1)}, u32[]{:S(2)}, u32[]{:S(2)}) collective-permute-start(f32[2,4,32,128]{3,2,1,0:T(8,128)S(1)} %get-tuple-element.38), channel_id=1, source_target_pairs={{0,4},{4,8},{8,12},{1,5},{5,9},{9,13},{2,6},{6,10},{10,14},{3,7},{... | collective-permute-start | bytes 393224 | tf_op jit(solution)/shard_map/ppermute | solution.py:16
  14.4 6.9 %collective-permute-start = (f32[2,4,32,128]{3,2,1,0:T(8,128)S(1)}, f32[2,4,32,128]{3,2,1,0:T(8,128)S(1)}, u32[]{:S(2)}, u32[]{:S(2)}) collective-permute-start(f32[2,4,32,128]{3,2,1,0:T(8,128)S(1)} %get-tuple-element.37), channel_id=1, source_target_pairs={{4,0},{8,4},{12,8},{5,1},{9,5},{13,9},{6,2},{10,6},{14,10},{7,3},{... | collective-permute-start | bytes 393224 | tf_op jit(solution)/shard_map/ppermute | solution.py:17
  22.9 7.1 %copy-start.13 = (f32[16]{0:T(128)S(1)}, f32[16]{0:T(128)}, u32[]{:S(2)}) copy-start(f32[16]{0:T(128)} %param.24) | copy-start | bytes 196
  24.9 13.4 %collective-permute-start.3 = (f32[2,40,32,4]{1,2,3,0:T(8,128)S(1)}, f32[2,40,32,4]{1,2,3,0:T(8,128)S(1)}, u32[]{:S(2)}, u32[]{:S(2)}) collective-permute-start(f32[2,40,32,4]{1,2,3,0:T(8,128)S(1)} %copy.34), channel_id=1, source_target_pairs={{1,0},{3,2},{5,4},{7,6},{9,8},{11,10},{13,12},{15,14},{17,16},{19,... | collective-permute-start | bytes 122888 | tf_op jit(solution)/shard_map/ppermute | solution.py:17
  27.0 12.4 %collective-permute-start.2 = (f32[2,40,32,4]{1,2,3,0:T(8,128)S(1)}, f32[2,40,32,4]{1,2,3,0:T(8,128)S(1)}, u32[]{:S(2)}, u32[]{:S(2)}) collective-permute-start(f32[2,40,32,4]{1,2,3,0:T(8,128)S(1)} %copy.33), channel_id=1, source_target_pairs={{0,1},{2,3},{4,5},{6,7},{8,9},{10,11},{12,13},{14,15},{16,17},{18,... | collective-permute-start | bytes 122888 | tf_op jit(solution)/shard_map/ppermute | solution.py:16
  37.5 0.8 copy-start.9
  41.6 4.6 %copy-start.3 = (f32[2,40,32,4]{3,2,1,0:T(8,128)S(1)}, f32[2,40,32,4]{3,2,1,0:T(8,128)}, u32[]{:S(2)}) copy-start(f32[2,40,32,4]{3,2,1,0:T(8,128)} %copy.35) | copy-start | bytes 122884
  48.3 10.4 %copy-start.5 = (f32[1,32,32,128]{3,2,1,0:T(8,128)S(1)}, f32[1,32,32,128]{3,2,1,0:T(8,128)}, u32[]{:S(2)}) copy-start(f32[1,32,32,128]{3,2,1,0:T(8,128)} %param.18) | copy-start | bytes 1572868
  48.3 10.4 %copy-start.8 = (f32[32,32,128]{2,1,0:T(8,128)S(1)}, f32[32,32,128]{2,1,0:T(8,128)}, u32[]{:S(2)}) copy-start(f32[32,32,128]{2,1,0:T(8,128)} %param.14) | copy-start | bytes 1572868
  58.7 3.8 %copy-start.4 = (f32[2,32,32,128]{3,2,1,0:T(8,128)}, f32[2,32,32,128]{3,2,1,0:T(8,128)S(1)}, u32[]{:S(2)}) copy-start(f32[2,32,32,128]{3,2,1,0:T(8,128)S(1)} %fusion.7) | copy-start | bytes 3145732
  62.4 44.6 %copy-start = (f32[1,32,32,128]{3,2,1,0:T(8,128)}, f32[1,32,32,128]{3,2,1,0:T(8,128)S(1)}, u32[]{:S(2)}) copy-start(f32[1,32,32,128]{3,2,1,0:T(8,128)S(1)} %get-tuple-element.24) | copy-start | bytes 1572868
  62.5 10.7 %collective-permute-start.4 = (f32[2,4,32,128]{3,2,1,0:T(8,128)S(1)}, f32[2,4,32,128]{3,2,1,0:T(8,128)S(1)}, u32[]{:S(2)}, u32[]{:S(2)}) collective-permute-start(f32[2,4,32,128]{3,2,1,0:T(8,128)S(1)} %get-tuple-element.36), channel_id=1, source_target_pairs={{4,0},{8,4},{12,8},{5,1},{9,5},{13,9},{6,2},{10,6},{14,10},{7,3},{... | collective-permute-start | bytes 393224 | tf_op jit(solution)/shard_map/ppermute | solution.py:17
  63.8 9.4 %collective-permute-start.5 = (f32[2,4,32,128]{3,2,1,0:T(8,128)S(1)}, f32[2,4,32,128]{3,2,1,0:T(8,128)S(1)}, u32[]{:S(2)}, u32[]{:S(2)}) collective-permute-start(f32[2,4,32,128]{3,2,1,0:T(8,128)S(1)} %get-tuple-element.35), channel_id=1, source_target_pairs={{0,4},{4,8},{8,12},{1,5},{5,9},{9,13},{2,6},{6,10},{10,14},{3,7},{... | collective-permute-start | bytes 393224 | tf_op jit(solution)/shard_map/ppermute | solution.py:16
  73.1 52.1 %reduce-scatter.3.cloned.1.call-start = ((), (), s32[]{:S(2)}) async-start(), calls=%async_computation.2 | async-start | bytes 786432 | tf_op jit(solution)/shard_map/reduce_scatter | solution.py:109
  73.2 0.7 copy-start.6
  78.1 8.3 %collective-permute-start.7 = (f32[2,40,32,4]{1,2,3,0:T(8,128)}, f32[2,40,32,4]{1,2,3,0:T(8,128)}, u32[]{:S(2)}, u32[]{:S(2)}) collective-permute-start(f32[2,40,32,4]{1,2,3,0:T(8,128)} %copy.40), channel_id=1, source_target_pairs={{1,0},{3,2},{5,4},{7,6},{9,8},{11,10},{13,12},{15,14},{17,16},{19,... | collective-permute-start | bytes 122888 | tf_op jit(solution)/shard_map/ppermute | solution.py:17
  80.8 8.6 %collective-permute-start.6 = (f32[2,40,32,4]{1,2,3,0:T(8,128)}, f32[2,40,32,4]{1,2,3,0:T(8,128)}, u32[]{:S(2)}, u32[]{:S(2)}) collective-permute-start(f32[2,40,32,4]{1,2,3,0:T(8,128)} %copy.39), channel_id=1, source_target_pairs={{0,1},{2,3},{4,5},{6,7},{8,9},{10,11},{12,13},{14,15},{16,17},{18,... | collective-permute-start | bytes 122888 | tf_op jit(solution)/shard_map/ppermute | solution.py:16
  92.4 4.0 %copy-start.1 = (f32[2,40,32,4]{3,2,1,0:T(8,128)S(1)}, f32[2,40,32,4]{3,2,1,0:T(8,128)}, u32[]{:S(2)}) copy-start(f32[2,40,32,4]{3,2,1,0:T(8,128)} %copy.42) | copy-start | bytes 122884
  92.4 4.0 %copy-start.2 = (f32[2,40,32,4]{3,2,1,0:T(8,128)S(1)}, f32[2,40,32,4]{3,2,1,0:T(8,128)}, u32[]{:S(2)}) copy-start(f32[2,40,32,4]{3,2,1,0:T(8,128)} %copy.41) | copy-start | bytes 122884
  92.4 4.0 %copy-start.7 = (f32[2,4,32,128]{3,2,1,0:T(8,128)S(1)}, f32[2,4,32,128]{3,2,1,0:T(8,128)}, u32[]{:S(2)}) copy-start(f32[2,4,32,128]{3,2,1,0:T(8,128)} %copy-done.6) | copy-start | bytes 393220
Sparse Core Ops, SparseCore 0:
  73.2 14.7 reduce-scatter.4
  110.4 14.7 reduce-scatter.2
where the time goes:
time: 134 us
  other arithmetic  54.9 us (41%)
  local copies, waits for them, and re-layouts  23 us (17%)
  starting transfers between devices  22.1 us (16%)
  between operations  17.1 us (13%)
  waiting for transfers between devices  16.8 us (13%)
    add x2, other arithmetic, laplace_padded(): summed = summed + STENCIL[offset] * (near_x + near_y + near_z)  17.8 us
    ppermute x4, starting transfers between devices, padded_2(): before = lax.ppermute(last, axis, up)  16.8 us
    concatenate x7, other arithmetic, padded_2(): x = jnp.concatenate([before, x, after], axis=dim)  15.3 us
    reduce_scatter x1, waiting for transfers between devices, shards(): lax.psum_scatter(early_grad, 'shot', scatter_dimension=1, tiled=True)  13.2 us
    scatter-add x3, other arithmetic, spread(): grid = jnp.zeros((shots_here * block_cells,), jnp.float32).at[target.resh...  9.53 us
    slice x5, local copies, waits for them, and re-layouts, padded_2(): initial = lax.slice_in_dim(x, 0, width, axis=dim)  7.78 us
    ppermute x2, local copies, waits for them, and re-layouts, padded_2(): before = lax.ppermute(last, axis, up)  5.15 us
    ppermute x4, starting transfers between devices, padded_2(): after = lax.ppermute(initial, axis, down)  5.15 us
  transfers between devices with their start and end apart: 10, of which 2 were waited for; matrix products, arithmetic and copies ran while one was open for 34% of the time, Pallas kernels for 0%

commit v1 on v0

v1 whole, which is shorter than its diff:
```python
import functools

import jax
import jax.numpy as jnp
import ml_dtypes
import numpy as np
from jax import lax
from jax.experimental import pallas as pl
from jax.experimental.pallas import tpu as pltpu
from jax.sharding import PartitionSpec as P

STENCIL = (-205.0 / 72.0, 8.0 / 5.0, -1.0 / 5.0, 8.0 / 315.0, -1.0 / 560.0)
HIGH = tuple(float(np.float32(c).astype(ml_dtypes.bfloat16)) for c in STENCIL)
LOW = tuple(float(np.float32(c - h).astype(ml_dtypes.bfloat16)) for c, h in zip(STENCIL, HIGH))
MESH = pl.DeviceIdType.MESH
PAD = 8
HALO = 4
ENERGY_CHUNKS = ((4, 16), (16, 28), (0, 4), (28, 32))
GRAD_CHUNKS = ((8, 16), (16, 24), (0, 8), (24, 32))


def kernel(
    sizes,
    courant_hbm, old_hbm, now_hbm, far_hbm, near_hbm,
    wavelet, source_cell, step, cells, residual, table, index,
    grad_hbm, energy_hbm, anow_hbm, aback_hbm,
    fpad, apad, fpad2, apad2, courant, old, far, zf, za, lapf, rec0, rec1, back,
    ebuf, gbuf, erecv, grecv, band, qsend, qrecv, hot,
    in_sem, out_sem, face_send, face_recv, zsend, zrecv, esend_sem, erecv_sem, gsend_sem, grecv_sem,
):
    tiles, shots, nx, ny, nz = sizes
    rows_y = ny // shots
    total_z = 2 * nz
    tile, shot, gz = (lax.axis_index(a) for a in ("tile", "shot", "gz"))
    y0, y1 = PAD, PAD + ny

    def inner(ref):
        return ref.at[HALO:HALO + nx, y0:y1, :]

    loads = [
        pltpu.make_async_copy(now_hbm.at[0], inner(fpad), in_sem.at[0]),
        pltpu.make_async_copy(near_hbm.at[0], inner(apad), in_sem.at[1]),
        pltpu.make_async_copy(old_hbm.at[0], old, in_sem.at[2]),
        pltpu.make_async_copy(courant_hbm, courant, in_sem.at[3]),
        pltpu.make_async_copy(far_hbm.at[0], far, in_sem.at[4]),
    ]
    for load in loads:
        load.start()

    barrier = pltpu.get_barrier_semaphore()
    pl.semaphore_signal(barrier, 1, device_id={"gz": 1 - gz}, device_id_type=MESH)
    for d in range(1, shots):
        pl.semaphore_signal(barrier, 1, device_id={"shot": lax.rem(shot + d, shots)}, device_id_type=MESH)

    @pl.when(tile > 0)
    def _():
        pl.semaphore_signal(barrier, 1, device_id={"tile": tile - 1}, device_id_type=MESH)

    @pl.when(tile < tiles - 1)
    def _():
        pl.semaphore_signal(barrier, 1, device_id={"tile": tile + 1}, device_id_type=MESH)

    for ref in (fpad, apad, fpad2, apad2):
        def clear(x, _, ref=ref):
            ref[x + HALO, 0:PAD, :] = jnp.zeros((PAD, nz), jnp.float32)
            ref[x + HALO, y1:y1 + PAD, :] = jnp.zeros((PAD, nz), jnp.float32)
            return 0
        lax.fori_loop(0, nx, clear, 0)

        @pl.when(tile == 0)
        def _():
            ref[0:HALO, y0:y1, :] = jnp.zeros((HALO, ny, nz), jnp.float32)

        @pl.when(tile == tiles - 1)
        def _():
            ref[HALO + nx:, y0:y1, :] = jnp.zeros((HALO, ny, nz), jnp.float32)

    ki = lax.broadcasted_iota(jnp.int32, (nz, nz), 0)
    kj = lax.broadcasted_iota(jnp.int32, (nz, nz), 1)
    dist = jnp.abs(ki - kj)
    upper = jnp.zeros((nz, nz), jnp.float32)
    lower = jnp.zeros((nz, nz), jnp.float32)
    for k in range(1, 5):
        upper = jnp.where(dist == k, HIGH[k], upper)
        lower = jnp.where(dist == k, LOW[k], lower)
    band[0:nz, 0:nz] = upper.astype(jnp.bfloat16)
    band[nz:2 * nz, 0:nz] = upper.astype(jnp.bfloat16)
    band[0:nz, nz:2 * nz] = lower.astype(jnp.bfloat16)
    band[nz:2 * nz, nz:2 * nz] = jnp.zeros((nz, nz), jnp.bfloat16)

    weight = table[index[0]] / shots
    amplitude = wavelet[step[0]]
    cell = source_cell[0]
    z_bits = total_z.bit_length() - 1
    y_bits = ny.bit_length() - 1
    src_row = lax.shift_right_logical(cell, z_bits)
    src_z = (cell & (total_z - 1)) - gz * nz
    src_y = src_row & (ny - 1)
    src_x = lax.shift_right_logical(src_row, y_bits) - tile * nx
    lane = lax.broadcasted_iota(jnp.int32, (ny, nz), 1)
    sub = lax.broadcasted_iota(jnp.int32, (ny, nz), 0)
    src_plane = jnp.where((sub == src_y) & (lane == src_z), amplitude, 0.0)
    first_edge = jnp.where(gz == 0, nz - HALO, 0)
    edge = (lane >= first_edge) & (lane < first_edge + HALO)
    quad = lax.shift_right_logical(lane, 2)
    place = lane & 3

    rc = cells[...]
    rec_row = lax.shift_right_logical(rc, z_bits) - tile * (nx * ny)
    rec_z = (rc & (total_z - 1)) - gz * nz
    nrec = rc.shape[1]
    z_hot = lax.broadcasted_iota(jnp.int32, (nz, nrec), 0) == rec_z
    for j in range(2):
        res = residual[0, j:j + 1, :]
        res_hi = res.astype(jnp.bfloat16).astype(jnp.float32)
        res_lo = res - res_hi
        hot[(2 * j) * nz:(2 * j + 1) * nz, :] = jnp.where(z_hot, res_hi, 0.0).astype(jnp.bfloat16)
        hot[(2 * j + 1) * nz:(2 * j + 2) * nz, :] = jnp.where(z_hot, res_lo, 0.0).astype(jnp.bfloat16)

    def face(n, ref, up):
        if up:
            src, dst, peer = ref.at[nx:nx + HALO, y0:y1, :], ref.at[0:HALO, y0:y1, :], tile + 1
        else:
            src, dst, peer = ref.at[HALO:2 * HALO, y0:y1, :], ref.at[HALO + nx:, y0:y1, :], tile - 1
        i = 2 * n + int(up)
        return pltpu.make_async_remote_copy(
            src_ref=src, dst_ref=dst, send_sem=face_send.at[i], recv_sem=face_recv.at[i],
            device_id={"tile": peer}, device_id_type=MESH)

    def send_faces(n, ref):
        @pl.when(tile < tiles - 1)
        def _():
            face(n, ref, True).start()

        @pl.when(tile > 0)
        def _():
            face(n, ref, False).start()

    def recv_faces(n, ref):
        @pl.when(tile > 0)
        def _():
            face(n, ref, True).wait_recv()

        @pl.when(tile < tiles - 1)
        def _():
            face(n, ref, False).wait_recv()

    def sent_faces(n, ref):
        @pl.when(tile < tiles - 1)
        def _():
            face(n, ref, True).wait_send()

        @pl.when(tile > 0)
        def _():
            face(n, ref, False).wait_send()

    def sides(n):
        return pltpu.make_async_remote_copy(
            src_ref=qsend.at[n], dst_ref=qrecv.at[n], send_sem=zsend.at[n], recv_sem=zrecv.at[n],
            device_id={"gz": 1 - gz}, device_id_type=MESH)

    def sums(buf, landing, send, recv, chunks, i, d):
        a, b = chunks[i]
        peer = lax.rem(shot + d, shots)
        return pltpu.make_async_remote_copy(
            src_ref=buf.at[peer, a:b], dst_ref=landing.at[d - 1, a:b],
            send_sem=send.at[i, d - 1], recv_sem=recv.at[i, d - 1],
            device_id={"shot": peer}, device_id_type=MESH)

    energy = functools.partial(sums, ebuf, erecv, esend_sem, erecv_sem, ENERGY_CHUNKS)
    grads = functools.partial(sums, gbuf, grecv, gsend_sem, grecv_sem, GRAD_CHUNKS)

    def pack(n, ref):
        def body(x, acc):
            plane = ref[x + HALO, y0:y1, :]
            turned = pltpu.roll(plane, (4 * x + jnp.where(gz == 0, 4, 0)) & (nz - 1), 1)
            return jnp.where(quad == x, turned, acc)
        packed = lax.fori_loop(0, nx, body, jnp.zeros((ny, nz), jnp.float32), unroll=4)
        total = STENCIL[4] * packed
        for d in range(1, 4):
            shift = jnp.where(gz == 1, d, nz - d)
            valid = jnp.where(gz == 1, place, 3 - place) >= d
            total = total + jnp.where(valid, STENCIL[4 - d] * pltpu.roll(packed, shift, 1), 0.0)
        qsend[n] = total
        sides(n).start()

    def along_z(ref, out, chunk=8):
        def body(i, _):
            x = i * chunk
            v = ref[pl.ds(HALO + x, chunk), y0:y1, :].reshape(chunk * ny, nz)
            hi = v.astype(jnp.bfloat16)
            lo = (v - hi.astype(jnp.float32)).astype(jnp.bfloat16)
            both = jnp.concatenate([hi, lo], axis=1)
            res = jnp.dot(both, band[...], preferred_element_type=jnp.float32)
            out[pl.ds(x, chunk)] = (res[:, :nz] + res[:, nz:]).reshape(chunk, ny, nz)
            return 0
        lax.fori_loop(0, nx // chunk, body, 0, unroll=2)

    def laplace(ref, zpart, q, x):
        centre = ref[x + HALO, y0:y1, :]
        turned = pltpu.roll(q, (first_edge - 4 * x + nz) & (nz - 1), 1)
        acc = zpart[x] + jnp.where(edge, turned, 0.0) + (3.0 * STENCIL[0]) * centre
        for k in range(1, 5):
            near = (ref[x + HALO - k, y0:y1, :] + ref[x + HALO + k, y0:y1, :]) + (
                ref[x + HALO, y0 - k:y1 - k, :] + ref[x + HALO, y0 + k:y1 + k, :])
            acc = acc + STENCIL[k] * near
        return acc, centre

    def planes(body, a, b):
        def step_fn(x, _):
            body(x)
            return 0
        lax.fori_loop(a, b, step_fn, 0, unroll=2)

    loads[0].wait()
    pl.semaphore_wait(
        barrier, shots + jnp.where(tile > 0, 1, 0) + jnp.where(tile < tiles - 1, 1, 0))

    send_faces(0, fpad)
    pack(0, fpad)
    loads[1].wait()
    send_faces(1, apad)
    pack(1, apad)
    along_z(fpad, zf)
    loads[2].wait()
    loads[3].wait()
    sides(0).wait_recv()
    q0 = qrecv[0]

    def forward(x):
        lap, now = laplace(fpad, zf, q0, x)
        lapf[x] = lap
        c = courant[x]
        src = src_plane * jnp.where(x == src_x, 1.0, 0.0)
        nxt = 2.0 * now - old[x] + (c * c) * (lap + src)
        fpad2[x + HALO, y0:y1, :] = nxt
        e = weight * (nxt * nxt + now * now)
        for s in range(shots):
            ebuf[s, x] = e[s * rows_y:(s + 1) * rows_y, :]

    for i in range(2):
        planes(forward, *ENERGY_CHUNKS[i])
        for d in range(1, shots):
            energy(i, d).start()
    recv_faces(0, fpad)
    for i in range(2, 4):
        planes(forward, *ENERGY_CHUNKS[i])
        for d in range(1, shots):
            energy(i, d).start()
    send_faces(2, fpad2)
    pack(2, fpad2)

    along_z(apad, za)
    chunk_rows = 256

    def receivers(i, _):
        base = i * chunk_rows
        row = lax.broadcasted_iota(jnp.int32, (chunk_rows, nrec), 0) + base
        row_hot = jnp.where(row == rec_row, 1.0, 0.0).astype(jnp.bfloat16)
        res = lax.dot_general(row_hot, hot[...], (((1,), (1,)), ((), ())), preferred_element_type=jnp.float32)
        px = chunk_rows // ny
        rec0[pl.ds(i * px, px)] = (res[:, :nz] + res[:, nz:2 * nz]).reshape(px, ny, nz)
        rec1[pl.ds(i * px, px)] = (res[:, 2 * nz:3 * nz] + res[:, 3 * nz:]).reshape(px, ny, nz)
        return 0

    lax.fori_loop(0, nx * ny // chunk_rows, receivers, 0)
    loads[4].wait()
    sides(1).wait_recv()
    recv_faces(1, apad)
    q1 = qrecv[1]

    def adjoint(x):
        lap, near = laplace(apad, za, q1, x)
        c = courant[x]
        apad2[x + HALO, y0:y1, :] = 2.0 * near - far[x] + (c * c) * (lap + rec0[x])

    planes(adjoint, 0, 4)
    planes(adjoint, nx - 4, nx)
    send_faces(3, apad2)
    planes(adjoint, 4, nx - 4)
    pack(3, apad2)
    store_now = pltpu.make_async_copy(inner(apad2), anow_hbm.at[0], out_sem.at[0])
    store_now.start()

    along_z(fpad2, zf)
    sides(2).wait_recv()
    q2 = qrecv[2]

    def gradient(x):
        lap, _ = laplace(fpad2, zf, q2, x)
        g = (2.0 * weight) * courant[x] * (
            apad[x + HALO, y0:y1, :] * lap + apad2[x + HALO, y0:y1, :] * lapf[x])
        for s in range(shots):
            gbuf[s, x] = g[s * rows_y:(s + 1) * rows_y, :]

    for i in range(2):
        planes(gradient, *GRAD_CHUNKS[i])
        for d in range(1, shots):
            grads(i, d).start()
    recv_faces(2, fpad2)
    for i in range(2, 4):
        planes(gradient, *GRAD_CHUNKS[i])
        for d in range(1, shots):
            grads(i, d).start()

    along_z(apad2, za)
    sides(3).wait_recv()
    recv_faces(3, apad2)
    q3 = qrecv[3]

    def adjoint_back(x):
        lap, now = laplace(apad2, za, q3, x)
        c = courant[x]
        back[x] = 2.0 * now - apad[x + HALO, y0:y1, :] + (c * c) * (lap + rec1[x])

    planes(adjoint_back, 0, nx)
    store_back = pltpu.make_async_copy(back, aback_hbm.at[0], out_sem.at[1])
    store_back.start()

    stores = []
    for n, (buf, landing, copies, chunks, out) in enumerate((
            (ebuf, erecv, energy, ENERGY_CHUNKS, energy_hbm),
            (gbuf, grecv, grads, GRAD_CHUNKS, grad_hbm))):
        for i, (a, b) in enumerate(chunks):
            for d in range(1, shots):
                copies(i, d).wait_recv()

            def total(x, buf=buf, landing=landing):
                acc = buf[shot, x]
                for d in range(1, shots):
                    acc = acc + landing[d - 1, x]
                landing[0, x] = acc

            planes(total, a, b)
            store = pltpu.make_async_copy(landing.at[0, a:b], out.at[a:b], out_sem.at[2 + 4 * n + i])
            store.start()
            stores.append(store)

    for n, ref in enumerate((fpad, apad, fpad2, apad2)):
        sent_faces(n, ref)
        sides(n).wait_send()
    for i in range(4):
        for d in range(1, shots):
            energy(i, d).wait_send()
            grads(i, d).wait_send()
    store_now.wait()
    store_back.wait()
    for store in stores:
        store.wait()


def shards(tiles, shots, *args):
    _, nx, ny, nz = args[2].shape
    nrec = args[8].shape[1]
    rows_y = ny // shots
    landings = max(shots - 1, 1)
    block = (nx, ny, nz)
    padded = (nx + 2 * HALO, ny + 2 * PAD, nz)
    f32 = jnp.float32
    anywhere = pl.BlockSpec(memory_space=pl.ANY)
    vmem = pl.BlockSpec(memory_space=pltpu.VMEM)
    smem = pl.BlockSpec(memory_space=pltpu.SMEM)
    dma = pltpu.SemaphoreType.DMA
    return pl.pallas_call(
        functools.partial(kernel, (tiles, shots, nx, ny, nz)),
        out_shape=(
            jax.ShapeDtypeStruct((nx, rows_y, nz), f32),
            jax.ShapeDtypeStruct((nx, rows_y, nz), f32),
            jax.ShapeDtypeStruct((1,) + block, f32),
            jax.ShapeDtypeStruct((1,) + block, f32),
        ),
        in_specs=[anywhere] * 5 + [smem] * 3 + [vmem] * 2 + [smem] * 2,
        out_specs=(anywhere,) * 4,
        scratch_shapes=(
            [pltpu.VMEM(padded, f32)] * 4
            + [pltpu.VMEM(block, f32)] * 9
            + [pltpu.VMEM((shots, nx, rows_y, nz), f32)] * 2
            + [pltpu.VMEM((landings, nx, rows_y, nz), f32)] * 2
            + [
                pltpu.VMEM((2 * nz, 2 * nz), jnp.bfloat16),
                pltpu.VMEM((4, ny, nz), f32),
                pltpu.VMEM((4, ny, nz), f32),
                pltpu.VMEM((4 * nz, nrec), jnp.bfloat16),
                dma((5,)), dma((10,)), dma((8,)), dma((8,)), dma((4,)), dma((4,)),
                dma((4, landings)), dma((4, landings)), dma((4, landings)), dma((4, landings)),
            ]
        ),
        compiler_params=pltpu.CompilerParams(
            collective_id=0, has_side_effects=True, vmem_limit_bytes=48 * 1024 * 1024),
        cost_estimate=pl.CostEstimate(
            flops=130 * nx * ny * nz, bytes_accessed=32 * nx * ny * nz, transcendentals=0),
        name="adjoint_window",
    )(*args)


def solution(mesh):
    wave = P(("grp", "shot"), "tile", None, "gz")
    one = P(("grp", "shot"))
    in_specs = (P("tile", None, "gz"), wave, wave, wave, wave, P(), one, one,
                P(("grp", "shot"), None), P(("grp", "shot"), None, None), P(), one)
    out_specs = (P(("grp", "tile"), "shot", "gz"), P(("grp", "tile"), "shot", "gz"), wave, wave)
    body = functools.partial(shards, mesh.shape["tile"], mesh.shape["shot"])
    return jax.shard_map(body, mesh=mesh, in_specs=in_specs, out_specs=out_specs, check_vma=False)
```

time: 134 us -> 33.5 us (0.25)
  other arithmetic: 54.9 us -> 0 us
  starting transfers between devices: 22.1 us -> 0 us
  Pallas kernels: 0 us -> 21.5 us
  waiting for transfers between devices: 16.8 us -> 0 us
  between operations: 17.1 us -> 2.67 us
  local copies, waits for them, and re-layouts: 23 us -> 8.89 us
    add x4 -> x0, other arithmetic: 24.8 us -> none  [the longest x2 17.8 us: laplace_padded(): summed = summed + STENCIL[offset] * (near_x + near_y + near_z)]
    ppermute x8 -> x0, starting transfers between devices: 22 us -> none  [the longest x4 16.8 us: padded_2(): before = lax.ppermute(last, axis, up)]
    pallas_call x0 -> x1, Pallas kernels: none -> 21.5 us  [shards(): pl.pallas_call(functools.partial(kernel, (tiles, shots, nx, ny, nz)), out...]
    concatenate x8 -> x0, other arithmetic: 15.3 us -> none  [the longest x7 15.3 us: padded_2(): x = jnp.concatenate([before, x, after], axis=dim)]
    reduce_scatter x2 -> x0, waiting for transfers between devices: 13.2 us -> none  [the longest x1 13.2 us: shards(): lax.psum_scatter(early_grad, 'shot', scatter_dimension=1, tiled=True)]
    slice x8 -> x0, local copies, waits for them, and re-layouts: 9.98 us -> none  [the longest x5 7.78 us: padded_2(): initial = lax.slice_in_dim(x, 0, width, axis=dim)]
    scatter-add x3 -> x0, other arithmetic: 9.53 us -> none  [spread(): grid = jnp.zeros((shots_here * block_cells,), jnp.float32).at[target.resh...]
    ppermute x4 -> x0, local copies, waits for them, and re-layouts: 9.29 us -> none  [the longest x2 5.15 us: padded_2(): before = lax.ppermute(last, axis, up)]
  transfers between devices with their start and end apart: 10 -> 0, of which waited for: 2 -> 0; matrix products, arithmetic and copies ran while one was open for 34% -> 0% of each run, Pallas kernels for 0% -> 0%
where the time goes in v1:
time: 33.5 us; the launch traced here: 33 us
  Pallas kernels  21.5 us (64%)
  local copies, waits for them, and re-layouts  8.89 us (27%)
  between operations  2.67 us (8%)
    pallas_call x1, Pallas kernels, shards(): pl.pallas_call(functools.partial(kernel, (tiles, shots, nx, ny, nz)), out...  21.5 us
    unnamed x22, local copies, waits for them, and re-layouts  8.89 us

profile of v1, /device:TPU:0, one launch (start us, length us, event | category | flops | bytes accessed | tf_op | source)
XLA Modules:
  0.0 33.0 jit_solution(2071007689295201865)
XLA Ops:
  0.6 0.0 copy-start.5
  1.9 0.0 copy-start.7
  2.0 0.0 copy-start.8
  2.6 0.0 copy-done.5
  2.6 0.0 copy-done.7
  2.7 0.0 copy-done.8
  2.7 0.0 copy-start
  2.7 1.0 %copy-done = f32[32,32,128]{2,1,0:T(8,128)S(1)} copy-done((f32[32,32,128]{2,1,0:T(8,128)S(1)}, f32[32,32,128]{2,1,0:T(8,128)}, u32[]{:S(2)}) %copy-start) | copy-done | bytes 524312
  3.7 0.0 copy-start.1
  3.7 1.0 %copy-done.1 = f32[1,32,32,128]{3,2,1,0:T(8,128)S(1)} copy-done((f32[1,32,32,128]{3,2,1,0:T(8,128)S(1)}, f32[1,32,32,128]{3,2,1,0:T(8,128)}, u32[]{:S(2)}) %copy-start.1) | copy-done | bytes 524312
  4.7 0.0 copy-start.2
  4.8 1.0 %copy-done.2 = f32[1,32,32,128]{3,2,1,0:T(8,128)S(1)} copy-done((f32[1,32,32,128]{3,2,1,0:T(8,128)S(1)}, f32[1,32,32,128]{3,2,1,0:T(8,128)}, u32[]{:S(2)}) %copy-start.2) | copy-done | bytes 524312
  5.8 0.0 copy-start.3
  5.8 1.0 %copy-done.3 = f32[1,32,32,128]{3,2,1,0:T(8,128)S(1)} copy-done((f32[1,32,32,128]{3,2,1,0:T(8,128)S(1)}, f32[1,32,32,128]{3,2,1,0:T(8,128)}, u32[]{:S(2)}) %copy-start.3) | copy-done | bytes 524312
  6.8 0.0 copy-start.4
  6.8 1.0 %copy-done.4 = f32[1,32,32,128]{3,2,1,0:T(8,128)S(1)} copy-done((f32[1,32,32,128]{3,2,1,0:T(8,128)S(1)}, f32[1,32,32,128]{3,2,1,0:T(8,128)}, u32[]{:S(2)}) %copy-start.4) | copy-done | bytes 524312
  7.9 0.0 copy-start.6
  7.9 0.7 %copy-done.6 = s32[1,512]{1,0:T(1,128)S(1)} copy-done((s32[1,512]{1,0:T(1,128)S(1)}, s32[1,512]{1,0:T(1,128)}, u32[]{:S(2)}) %copy-start.6) | copy-done | bytes 2072
  8.6 21.5 %adjoint_window.1 = (f32[32,16,128]{2,1,0:T(8,128)S(1)}, f32[32,16,128]{2,1,0:T(8,128)S(1)}, f32[1,32,32,128]{3,2,1,0:T(8,128)S(1)}, f32[1,32,32,128]{3,2,1,0:T(8,128)S(1)}) custom-call(f32[32,32,128]{2,1,0:T(8,128)S(1)} %copy-done, f32[1,32,32,128]{3,2,1,0:T(8,128)S(1)} %copy-done.1, f32[1,32,32,128]{3,2,1,0:T(8,128)S(1)} %copy-done.2, ...), custom_call_target="tpu_custom_call" | custom-call | flops 17039360 | bytes 4194304 | tf_op jit(solution)/shard_map/adjoint_window/pallas_call | solution.py:364
  30.1 0.7 %copy.23 = f32[32,16,128]{2,1,0:T(8,128)} copy(f32[32,16,128]{2,1,0:T(8,128)S(1)} %get-tuple-element.8) | data formatting | bytes 524288
  30.8 0.7 %copy.24 = f32[32,16,128]{2,1,0:T(8,128)} copy(f32[32,16,128]{2,1,0:T(8,128)S(1)} %get-tuple-element.9) | data formatting | bytes 524288
  31.5 0.8 %copy.25 = f32[1,32,32,128]{3,2,1,0:T(8,128)} copy(f32[1,32,32,128]{3,2,1,0:T(8,128)S(1)} %get-tuple-element.10) | data formatting | bytes 1048576
  32.3 0.8 %copy.26 = f32[1,32,32,128]{3,2,1,0:T(8,128)} copy(f32[1,32,32,128]{3,2,1,0:T(8,128)S(1)} %get-tuple-element.11) | data formatting | bytes 1048576
Async XLA Ops:
  0.6 2.0 %copy-start.5 = (f32[1,2,512]{2,1,0:T(2,128)S(1)}, f32[1,2,512]{2,1,0:T(2,128)}, u32[]{:S(2)}) copy-start(f32[1,2,512]{2,1,0:T(2,128)} %residual.1) | copy-start | bytes 12292
  1.9 0.7 %copy-start.7 = (f32[256]{0:T(256)S(1)}, f32[256]{0:T(256)}, u32[]{:S(2)}) copy-start(f32[256]{0:T(256)} %wavelet.1) | copy-start | bytes 3076
  2.0 0.7 %copy-start.8 = (f32[16]{0:T(128)S(1)}, f32[16]{0:T(128)}, u32[]{:S(2)}) copy-start(f32[16]{0:T(128)} %table.1) | copy-start | bytes 196
  2.7 1.0 %copy-start = (f32[32,32,128]{2,1,0:T(8,128)S(1)}, f32[32,32,128]{2,1,0:T(8,128)}, u32[]{:S(2)}) copy-start(f32[32,32,128]{2,1,0:T(8,128)} %courant_hbm.1) | copy-start | bytes 1572868
  3.7 1.0 %copy-start.1 = (f32[1,32,32,128]{3,2,1,0:T(8,128)S(1)}, f32[1,32,32,128]{3,2,1,0:T(8,128)}, u32[]{:S(2)}) copy-start(f32[1,32,32,128]{3,2,1,0:T(8,128)} %old_hbm.1) | copy-start | bytes 1572868
  4.7 1.0 %copy-start.2 = (f32[1,32,32,128]{3,2,1,0:T(8,128)S(1)}, f32[1,32,32,128]{3,2,1,0:T(8,128)}, u32[]{:S(2)}) copy-start(f32[1,32,32,128]{3,2,1,0:T(8,128)} %now_hbm.1) | copy-start | bytes 1572868
  5.8 1.0 %copy-start.3 = (f32[1,32,32,128]{3,2,1,0:T(8,128)S(1)}, f32[1,32,32,128]{3,2,1,0:T(8,128)}, u32[]{:S(2)}) copy-start(f32[1,32,32,128]{3,2,1,0:T(8,128)} %far_hbm.1) | copy-start | bytes 1572868
  6.8 1.0 %copy-start.4 = (f32[1,32,32,128]{3,2,1,0:T(8,128)S(1)}, f32[1,32,32,128]{3,2,1,0:T(8,128)}, u32[]{:S(2)}) copy-start(f32[1,32,32,128]{3,2,1,0:T(8,128)} %near_hbm.1) | copy-start | bytes 1572868
  7.9 0.7 %copy-start.6 = (s32[1,512]{1,0:T(1,128)S(1)}, s32[1,512]{1,0:T(1,128)}, u32[]{:S(2)}) copy-start(s32[1,512]{1,0:T(1,128)} %cells.1) | copy-start | bytes 6148

commit v2 on v1

--- a/solution.py
+++ b/solution.py
@@ -22,10 +22,11 @@
 def kernel(
     sizes,
     courant_hbm, old_hbm, now_hbm, far_hbm, near_hbm,
-    wavelet, source_cell, step, cells, residual, table, index,
+    wavelet_hbm, scalars_hbm, cells_hbm, residual_hbm, table_hbm,
     grad_hbm, energy_hbm, anow_hbm, aback_hbm,
     fpad, apad, fpad2, apad2, courant, old, far, zf, za, lapf, rec0, rec1, back,
     ebuf, gbuf, erecv, grecv, band, qsend, qrecv, hot,
+    wavelet, scalars, cells, residual, table,
     in_sem, out_sem, face_send, face_recv, zsend, zrecv, esend_sem, erecv_sem, gsend_sem, grecv_sem,
 ):
     tiles, shots, nx, ny, nz = sizes
@@ -44,7 +45,13 @@
         pltpu.make_async_copy(courant_hbm, courant, in_sem.at[3]),
         pltpu.make_async_copy(far_hbm.at[0], far, in_sem.at[4]),
     ]
-    for load in loads:
+    small = [
+        pltpu.make_async_copy(src, dst, in_sem.at[5 + i])
+        for i, (src, dst) in enumerate((
+            (wavelet_hbm, wavelet), (scalars_hbm, scalars), (cells_hbm, cells),
+            (residual_hbm, residual), (table_hbm, table)))
+    ]
+    for load in loads[:2] + small + loads[2:]:
         load.start()
 
     barrier = pltpu.get_barrier_semaphore()
@@ -65,7 +72,7 @@
             ref[x + HALO, 0:PAD, :] = jnp.zeros((PAD, nz), jnp.float32)
             ref[x + HALO, y1:y1 + PAD, :] = jnp.zeros((PAD, nz), jnp.float32)
             return 0
-        lax.fori_loop(0, nx, clear, 0)
+        lax.fori_loop(0, nx, clear, 0, unroll=8)
 
         @pl.when(tile == 0)
         def _():
@@ -88,9 +95,11 @@
     band[0:nz, nz:2 * nz] = lower.astype(jnp.bfloat16)
     band[nz:2 * nz, nz:2 * nz] = jnp.zeros((nz, nz), jnp.bfloat16)
 
-    weight = table[index[0]] / shots
-    amplitude = wavelet[step[0]]
-    cell = source_cell[0]
+    for load in small:
+        load.wait()
+    weight = table[scalars[2]] / shots
+    amplitude = wavelet[scalars[1]]
+    cell = scalars[0]
     z_bits = total_z.bit_length() - 1
     y_bits = ny.bit_length() - 1
     src_row = lax.shift_right_logical(cell, z_bits)
@@ -175,7 +184,7 @@
             plane = ref[x + HALO, y0:y1, :]
             turned = pltpu.roll(plane, (4 * x + jnp.where(gz == 0, 4, 0)) & (nz - 1), 1)
             return jnp.where(quad == x, turned, acc)
-        packed = lax.fori_loop(0, nx, body, jnp.zeros((ny, nz), jnp.float32), unroll=4)
+        packed = lax.fori_loop(0, nx, body, jnp.zeros((ny, nz), jnp.float32), unroll=16)
         total = STENCIL[4] * packed
         for d in range(1, 4):
             shift = jnp.where(gz == 1, d, nz - d)
@@ -194,7 +203,7 @@
             res = jnp.dot(both, band[...], preferred_element_type=jnp.float32)
             out[pl.ds(x, chunk)] = (res[:, :nz] + res[:, nz:]).reshape(chunk, ny, nz)
             return 0
-        lax.fori_loop(0, nx // chunk, body, 0, unroll=2)
+        lax.fori_loop(0, nx // chunk, body, 0, unroll=4)
 
     def laplace(ref, zpart, q, x):
         centre = ref[x + HALO, y0:y1, :]
@@ -210,7 +219,7 @@
         def step_fn(x, _):
             body(x)
             return 0
-        lax.fori_loop(a, b, step_fn, 0, unroll=2)
+        lax.fori_loop(a, b, step_fn, 0, unroll=4)
 
     loads[0].wait()
     pl.semaphore_wait(
@@ -263,7 +272,7 @@
         rec1[pl.ds(i * px, px)] = (res[:, 2 * nz:3 * nz] + res[:, 3 * nz:]).reshape(px, ny, nz)
         return 0
 
-    lax.fori_loop(0, nx * ny // chunk_rows, receivers, 0)
+    lax.fori_loop(0, nx * ny // chunk_rows, receivers, 0, unroll=2)
     loads[4].wait()
     sides(1).wait_recv()
     recv_faces(1, apad)
@@ -349,6 +358,19 @@
         store.wait()
 
 
+def write_out(*refs):
+    ins, outs, held, sem = refs[:4], refs[4:8], refs[8:12], refs[12]
+    first = [pltpu.make_async_copy(ins[i], held[i], sem.at[i]) for i in range(4)]
+    second = [pltpu.make_async_copy(held[i], outs[i], sem.at[4 + i]) for i in range(4)]
+    for copy in first:
+        copy.start()
+    for arrive, leave in zip(first, second):
+        arrive.wait()
+        leave.start()
+    for copy in second:
+        copy.wait()
+
+
 def shards(tiles, shots, *args):
     _, nx, ny, nz = args[2].shape
     nrec = args[8].shape[1]
@@ -358,10 +380,10 @@
     padded = (nx + 2 * HALO, ny + 2 * PAD, nz)
     f32 = jnp.float32
     anywhere = pl.BlockSpec(memory_space=pl.ANY)
-    vmem = pl.BlockSpec(memory_space=pltpu.VMEM)
-    smem = pl.BlockSpec(memory_space=pltpu.SMEM)
+    pinned = pl.BlockSpec(memory_space=pltpu.HBM)
     dma = pltpu.SemaphoreType.DMA
-    return pl.pallas_call(
+    scalars = jnp.concatenate([args[6], args[7], args[11]])
+    held = pl.pallas_call(
         functools.partial(kernel, (tiles, shots, nx, ny, nz)),
         out_shape=(
             jax.ShapeDtypeStruct((nx, rows_y, nz), f32),
@@ -369,7 +391,7 @@
             jax.ShapeDtypeStruct((1,) + block, f32),
             jax.ShapeDtypeStruct((1,) + block, f32),
         ),
-        in_specs=[anywhere] * 5 + [smem] * 3 + [vmem] * 2 + [smem] * 2,
+        in_specs=[pinned] * 10,
         out_specs=(anywhere,) * 4,
         scratch_shapes=(
             [pltpu.VMEM(padded, f32)] * 4
@@ -381,16 +403,31 @@
                 pltpu.VMEM((4, ny, nz), f32),
                 pltpu.VMEM((4, ny, nz), f32),
                 pltpu.VMEM((4 * nz, nrec), jnp.bfloat16),
-                dma((5,)), dma((10,)), dma((8,)), dma((8,)), dma((4,)), dma((4,)),
+                pltpu.SMEM(args[5].shape, f32),
+                pltpu.SMEM((3,), jnp.int32),
+                pltpu.VMEM(args[8].shape, jnp.int32),
+                pltpu.VMEM(args[9].shape, f32),
+                pltpu.SMEM(args[10].shape, f32),
+                dma((12,)), dma((10,)), dma((8,)), dma((8,)), dma((4,)), dma((4,)),
                 dma((4, landings)), dma((4, landings)), dma((4, landings)), dma((4, landings)),
             ]
         ),
         compiler_params=pltpu.CompilerParams(
-            collective_id=0, has_side_effects=True, vmem_limit_bytes=48 * 1024 * 1024),
+            collective_id=0, has_side_effects=True, vmem_limit_bytes=60 * 1024 * 1024),
         cost_estimate=pl.CostEstimate(
             flops=130 * nx * ny * nz, bytes_accessed=32 * nx * ny * nz, transcendentals=0),
         name="adjoint_window",
-    )(*args)
+    )(*args[:6], scalars, *args[8:11])
+    return pl.pallas_call(
+        write_out,
+        out_shape=tuple(jax.ShapeDtypeStruct(h.shape, f32) for h in held),
+        in_specs=[anywhere] * 4,
+        out_specs=(pinned,) * 4,
+        scratch_shapes=[pltpu.VMEM(h.shape, f32) for h in held] + [dma((8,))],
+        compiler_params=pltpu.CompilerParams(vmem_limit_bytes=60 * 1024 * 1024),
+        cost_estimate=pl.CostEstimate(flops=0, bytes_accessed=24 * nx * ny * nz, transcendentals=0),
+        name="write_out",
+    )(*held)
 
 
 def solution(mesh):

time: 33.5 us -> 25.3 us (0.76)
  local copies, waits for them, and re-layouts: 8.89 us -> 0 us
  other arithmetic: 0 us -> 0.59 us
  Pallas kernels: 21.5 us -> 21.9 us
    unnamed x22 -> x0, local copies, waits for them, and re-layouts: 8.89 us -> none
    pallas_call x0 -> x1, Pallas kernels: none -> 2.24 us  [shards(): pl.pallas_call(write_out, out_shape=tuple((jax.ShapeDtypeStruct(h.shape,...]
    pallas_call x1, Pallas kernels: 21.5 us -> 19.7 us  [shards(): pl.pallas_call(functools.partial(kernel, (tiles, shots, nx, ny, nz)), out...]
    concatenate x0 -> x1, other arithmetic: none -> 0.59 us  [shards(): scalars = jnp.concatenate([args[6], args[7], args[11]])]
where the time goes in v2:
time: 25.3 us; the launch traced here: 25.1 us
  Pallas kernels  21.9 us (87%)
  between operations  2.58 us (10%)
  other arithmetic  0.59 us (2%)
    pallas_call x1, Pallas kernels, shards(): pl.pallas_call(functools.partial(kernel, (tiles, shots, nx, ny, nz)), out...  19.7 us
    pallas_call x1, Pallas kernels, shards(): pl.pallas_call(write_out, out_shape=tuple((jax.ShapeDtypeStruct(h.shape,...  2.24 us
    concatenate x1, other arithmetic, shards(): scalars = jnp.concatenate([args[6], args[7], args[11]])  0.59 us

profile of v2, /device:TPU:0, one launch (start us, length us, event | category | flops | bytes accessed | tf_op | source)
XLA Modules:
  0.0 25.1 jit_solution(15190171478413167143)
XLA Ops:
  2.6 0.6 %pad_add_fusion.scalars_hbm = s32[3]{0:T(128)} fusion(s32[1]{0:T(128)S(6)} %copy.18, s32[1]{0:T(128)S(6)} %copy.17, s32[1]{0:T(128)S(6)} %copy.16), kind=kLoop, calls=%fused_computation | loop fusion | flops 6 | bytes 24 | tf_op jit(solution)/shard_map/concatenate | solution.py:385
  3.2 19.7 %adjoint_window.1 = (f32[32,16,128]{2,1,0:T(8,128)}, f32[32,16,128]{2,1,0:T(8,128)}, f32[1,32,32,128]{3,2,1,0:T(8,128)}, f32[1,32,32,128]{3,2,1,0:T(8,128)}) custom-call(f32[32,32,128]{2,1,0:T(8,128)} %courant_hbm.1, f32[1,32,32,128]{3,2,1,0:T(8,128)} %old_hbm.1, f32[1,32,32,128]{3,2,1,0:T(8,128)} %now_hbm.1, f32[1,32,32,128]{3,2,1,0:T(8,128)} %far_hbm.1, ...), custom_call_target="tpu_custom_call" | custom-call | flops 17039360 | bytes 4194304 | tf_op jit(solution)/shard_map/adjoint_window/pallas_call | solution.py:386
  22.8 2.2 %write_out.1 = (f32[32,16,128]{2,1,0:T(8,128)}, f32[32,16,128]{2,1,0:T(8,128)}, f32[1,32,32,128]{3,2,1,0:T(8,128)}, f32[1,32,32,128]{3,2,1,0:T(8,128)}) custom-call(f32[32,16,128]{2,1,0:T(8,128)} %get-tuple-element.8.refs_0_, f32[32,16,128]{2,1,0:T(8,128)} %get-tuple-element.9.refs_1_, f32[1,32,32,128]{3,2,1,0:T(8,128)} %get-tuple-element.10.refs_2_, ...), custom_call_target="tpu_custom_call" | custom-call | bytes 3145728 | tf_op jit(solution)/shard_map/write_out/pallas_call | solution.py:421
